TPU v7x, 32 devices: a whole 2x2x4 slice. The times are simulated.
32 devices in a mesh: tm: 2 (over x), height: 16 (over z, y, core).
Axes of the slice: x: 2, y: 2, z: 4, core: 2. Of those that a mesh axis runs over, the one named last changes fastest.
Arguments:
- features: bfloat16 [96, 8, 64, 128], P(None, 'tm', 'height'), may hold values from -6 to 6
- first_gain: float32 [96], replicated, may hold values from 0.1 to 1.9
- first_weight: bfloat16 [96, 2592], replicated, may hold values from -0.125 to 0.125
- first_bias: float32 [96], replicated, may hold values from -3 to 3
- second_gain: float32 [96], replicated, may hold values from 0.1 to 1.9
- second_weight: bfloat16 [96, 2592], replicated, may hold values from -0.125 to 0.125
- second_bias: float32 [96], replicated, may hold values from -3 to 3
Outputs:
- encoded: bfloat16 [96, 8, 64, 128], P(None, 'tm', 'height')
All inputs are finite; a program needn't handle non-finite values.
Results may differ from a plain program's by a relative error of at most 0.0036.
Values may be sent and summed in bfloat16 or wider, within the bound.
A program may use at most 64 MiB of HBM per device.

v0:
```python
import functools

import jax
import jax.numpy as jnp
from jax import lax
from jax.experimental import pallas as pl
from jax.experimental.pallas import tpu as pltpu
from jax.sharding import PartitionSpec as P

MESH = pl.DeviceIdType.MESH

def activate(values, gain):
    mean_square = jnp.mean(values * values, axis=0, keepdims=True)
    scaled = values * lax.rsqrt(mean_square + 1e-06) * gain
    return scaled * (0.5 + 0.5 * jnp.tanh(0.5 * scaled))


def spread(taps, frame, row, values):
    values = values.astype(jnp.bfloat16)
    lanes = lax.broadcasted_iota(jnp.int32, values.shape, 1)
    last = values.shape[1] - 1
    zero = jnp.zeros_like(values)
    taps[frame, row, 0] = jnp.where(lanes == 0, zero, pltpu.roll(values, 1, 1))
    taps[frame, row, 1] = values
    taps[frame, row, 2] = jnp.where(lanes == last, zero, pltpu.roll(values, last, 1))


def padded_width(width):
    return -(-width // 128) * 128


def window(taps, frame, pair):
    width, columns = 9 * taps.shape[3], taps.shape[4]
    zero = jnp.zeros((padded_width(width) - width, len(pair) * columns), taps.dtype)
    blocks = []
    for i in range(2):
        rows = [taps[frame + i, pl.ds(r, 3)].reshape(width, columns) for r in pair]
        blocks += [jnp.concatenate(rows, axis=1), zero]
    return jnp.concatenate(blocks, axis=0)


def multiply(weights, taps, frame, pair):
    return jnp.dot(weights, window(taps, frame, pair), preferred_element_type=jnp.float32)


def stack(weights, source):
    channels = source.shape[0]
    width = source.shape[1] // 3
    full = padded_width(width)
    zero = jnp.zeros((channels, full - width), source.dtype)
    early, middle, late = (
        jnp.concatenate([source[:, p * width : (p + 1) * width], zero], axis=1) for p in range(3)
    )
    none = jnp.zeros_like(early)
    for i, blocks in enumerate(((late, none), (middle, late), (early, middle), (none, early))):
        for j, block in enumerate(blocks):
            weights[i * channels : (i + 1) * channels, j * full : (j + 1) * full] = block


def column(vectors, i, columns):
    wide = jnp.broadcast_to(vectors[i], (columns, vectors.shape[2]))
    return jnp.transpose(wide)


def kernel(
    tm_count,
    height_count,
    features,
    first_weight_hbm,
    second_weight_hbm,
    first_gain_hbm,
    first_bias_hbm,
    second_gain_hbm,
    second_bias_hbm,
    out,
    vectors,
    first_weight,
    second_weight,
    weights_a,
    weights_b,
    own,
    above,
    below,
    earlier,
    earlier_above,
    earlier_below,
    taps_a,
    taps_b,
    total,
    send_sem,
    recv_sem,
    load_sem,
):
    loads = [
        pltpu.make_async_copy(source, target, load_sem.at[i])
        for i, (source, target) in enumerate(
            (
                (first_gain_hbm, vectors.at[0]),
                (first_bias_hbm, vectors.at[1]),
                (second_gain_hbm, vectors.at[2]),
                (second_bias_hbm, vectors.at[3]),
                (first_weight_hbm, first_weight),
                (second_weight_hbm, second_weight),
            )
        )
    ]
    for load in loads:
        load.start()
    t = lax.axis_index("tm")
    h = lax.axis_index("height")
    has_prev, has_next = t > 0, t < tm_count - 1
    has_up, has_down = h > 0, h < height_count - 1
    up, down = (t, h - 1), (t, h + 1)
    later = (t + 1, h)

    barrier = pltpu.get_barrier_semaphore()
    neighbours = (
        (has_prev, (t - 1, h)),
        (has_next, later),
        (has_up, up),
        (has_down, down),
    )
    for present, device in neighbours:

        @pl.when(present)
        def _():
            pl.semaphore_signal(barrier, inc=1, device_id=device, device_id_type=MESH)

    def message(layer, slot, source, target, device):
        return pltpu.make_async_remote_copy(
            src_ref=source,
            dst_ref=target,
            send_sem=send_sem.at[layer, slot],
            recv_sem=recv_sem.at[layer, slot],
            device_id=device,
            device_id_type=MESH,
        )

    def to_up(layer, half):
        frames = pl.ds(2 * half, 2)
        return message(
            layer, half, own.at[layer, frames, 0], below.at[layer, frames], up
        )

    def to_down(layer, half):
        frames = pl.ds(2 * half, 2)
        return message(
            layer, 2 + half, own.at[layer, frames, 3], above.at[layer, frames], down
        )

    def to_later(layer, part):
        row, count = ((0, 1), (3, 1), (1, 2))[part]
        rows = pl.ds(row, count)
        return message(
            layer,
            4 + part,
            own.at[layer, pl.ds(2, 2), rows],
            earlier.at[layer, :, rows],
            later,
        )

    def pass_up(layer):
        return message(layer, 7, earlier.at[layer, :, 0], earlier_below.at[layer], up)

    def pass_down(layer):
        return message(layer, 8, earlier.at[layer, :, 3], earlier_above.at[layer], down)

    def send_rows(layer, half):
        @pl.when(has_up)
        def _():
            to_up(layer, half).start()

        @pl.when(has_down)
        def _():
            to_down(layer, half).start()

    def send_later(layer, parts):
        @pl.when(has_next)
        def _():
            for part in parts:
                to_later(layer, part).start()

    def clear(taps, frames, row):
        for frame in frames:
            taps[frame, row] = jnp.zeros(taps.shape[2:], taps.dtype)

    def spread_frames(taps, first, row, source):
        def step(f, carry):
            spread(taps, first + f, row, source[f])
            return carry

        lax.fori_loop(0, 2, step, 0)

    def take_rows(layer, taps, half):
        frames = pl.ds(2 * half, 2)

        @pl.when(has_up)
        def _():
            to_down(layer, half).wait_recv()
            spread_frames(taps, 2 + 2 * half, 0, above.at[layer, frames])

        @pl.when(has_down)
        def _():
            to_up(layer, half).wait_recv()
            spread_frames(taps, 2 + 2 * half, 5, below.at[layer, frames])

    def clear_edges(taps):
        @pl.when(jnp.logical_not(has_up))
        def _():
            clear(taps, range(6), 0)

        @pl.when(jnp.logical_not(has_down))
        def _():
            clear(taps, range(6), 5)

    def pass_on(layer):
        @pl.when(has_prev)
        def _():
            to_later(layer, 0).wait_recv()

            @pl.when(has_up)
            def _():
                pass_up(layer).start()

            to_later(layer, 1).wait_recv()

            @pl.when(has_down)
            def _():
                pass_down(layer).start()

    def take_earlier(layer, taps):
        to_later(layer, 2).wait_recv()

        def step(f, carry):
            for r in range(4):
                spread(taps, f, r + 1, earlier[layer, f, r])
            return carry

        lax.fori_loop(0, 2, step, 0)

    def take_corners(layer, taps):
        @pl.when(has_up)
        def _():
            pass_down(layer).wait_recv()
            spread_frames(taps, 0, 0, earlier_above.at[layer])

        @pl.when(has_down)
        def _():
            pass_up(layer).wait_recv()
            spread_frames(taps, 0, 5, earlier_below.at[layer])

    def each_pair(step):
        def body(k, carry):
            step(k, (1 - k, 2 + k))
            return carry

        lax.fori_loop(0, 2, body, 0)

    def cut(part, i, j):
        return part[i * channels : (i + 1) * channels, j * columns : (j + 1) * columns]

    def plus_bias(part, bias):
        wide = jnp.concatenate([bias, bias], axis=1)
        return part + jnp.concatenate([wide, wide], axis=0)

    channels, columns = features.shape[2:]
    two = 2 * channels
    for load in loads[:4]:
        load.wait()
    first_gain, first_bias, second_gain, second_bias = (
        column(vectors, i, columns) for i in range(4)
    )

    def first_activation(f, carry):
        for r in range(4):
            act = activate(features[f, r].astype(jnp.float32), first_gain)
            own[0, f, r] = act.astype(jnp.bfloat16)
            spread(taps_a, f + 2, r + 1, act)
        return carry

    lax.fori_loop(0, 4, first_activation, 0)

    pl.semaphore_wait(
        barrier,
        sum(present.astype(jnp.int32) for present, _ in neighbours),
    )
    send_rows(0, 1)
    send_rows(0, 0)
    send_later(0, (0, 1, 2))

    loads[4].wait()
    stack(weights_a, first_weight)
    clear_edges(taps_a)
    clear_edges(taps_b)

    def second_activation(first, pair, part):
        for i in range(2):
            for j, r in enumerate(pair):
                act = activate(cut(part, i, j), second_gain)
                own[1, first + i, r] = act.astype(jnp.bfloat16)
                spread(taps_b, first + i + 2, r + 1, act)

    def finish(first, pair, part):
        for i in range(2):
            for j, r in enumerate(pair):
                value = features[first + i, r].astype(jnp.float32) + cut(part, i, j)
                out[first + i, r] = value.astype(jnp.bfloat16)

    def first_late(k, pair):
        @pl.when(k == 1)
        def _():
            take_rows(0, taps_a, 1)
            take_rows(0, taps_a, 0)

        part = multiply(weights_a[two:, :], taps_a, 2, pair)
        part = part + multiply(weights_a[:two, :], taps_a, 4, pair)
        second_activation(2, pair, plus_bias(part, first_bias))

        @pl.when(k == 0)
        def _():
            send_later(1, (2,))

    each_pair(first_late)
    send_later(1, (0, 1))
    send_rows(1, 1)
    pass_on(0)

    def first_early(k, pair):
        total[0, k] = plus_bias(multiply(weights_a[:two, :], taps_a, 2, pair), first_bias)

    each_pair(first_early)

    loads[5].wait()
    stack(weights_b, second_weight)

    def second_late(k, pair):
        total[1, k] = plus_bias(multiply(weights_b[:two, :], taps_b, 4, pair), second_bias)

    second_late(0, (1, 2))

    @pl.when(has_prev)
    def _():
        take_earlier(0, taps_a)

    def first_earlier(k, pair):
        @pl.when(has_prev)
        def _():
            @pl.when(k == 1)
            def _():
                take_corners(0, taps_a)

            total[0, k] += multiply(weights_a[two:, :], taps_a, 0, pair)

        second_activation(0, pair, total[0, k])

    each_pair(first_earlier)
    send_rows(1, 0)
    take_rows(1, taps_b, 1)
    second_late(1, (0, 3))

    def second_early(k, pair):
        @pl.when(k == 1)
        def _():
            pass_on(1)
            take_rows(1, taps_b, 0)

        part = multiply(weights_b[...], taps_b, 2, pair)
        finish(2, pair, total[1, k] + part[two:, :])
        total[0, k] = plus_bias(part[:two, :], second_bias)

    each_pair(second_early)

    @pl.when(has_prev)
    def _():
        take_earlier(1, taps_b)

    def second_earlier(k, pair):
        @pl.when(has_prev)
        def _():
            @pl.when(k == 1)
            def _():
                take_corners(1, taps_b)

            total[0, k] += multiply(weights_b[two:, :], taps_b, 0, pair)

        finish(0, pair, total[0, k])

    each_pair(second_earlier)

    for layer in range(2):

        @pl.when(has_up)
        def _():
            for half in range(2):
                to_up(layer, half).wait_send()

        @pl.when(has_down)
        def _():
            for half in range(2):
                to_down(layer, half).wait_send()

        @pl.when(has_next)
        def _():
            for part in range(3):
                to_later(layer, part).wait_send()

        @pl.when(has_prev & has_up)
        def _():
            pass_up(layer).wait_send()

        @pl.when(has_prev & has_down)
        def _():
            pass_down(layer).wait_send()


def local(features, first_gain, first_weight, first_bias, second_gain, second_weight, second_bias):
    channels, frames, rows, columns = features.shape
    by_row = jnp.transpose(features, (1, 2, 0, 3))
    vectors = [v.reshape(1, channels) for v in (first_gain, first_bias, second_gain, second_bias)]
    vmem = pl.BlockSpec(memory_space=pltpu.VMEM)
    act = jnp.bfloat16
    stacked = (4 * channels, 2 * padded_width(first_weight.shape[1] // 3))
    cells = 2 * channels * first_weight.shape[1] * frames * rows * columns
    result = pl.pallas_call(
        functools.partial(kernel, lax.axis_size("tm"), lax.axis_size("height")),
        out_shape=jax.ShapeDtypeStruct(by_row.shape, jnp.bfloat16),
        in_specs=[vmem] + [pl.BlockSpec(memory_space=pltpu.HBM)] * 6,
        out_specs=vmem,
        scratch_shapes=[
            pltpu.VMEM((4, 1, channels), jnp.float32),
            pltpu.VMEM(first_weight.shape, act),
            pltpu.VMEM(second_weight.shape, act),
            pltpu.VMEM(stacked, act),
            pltpu.VMEM(stacked, act),
            pltpu.VMEM((2, frames, rows, channels, columns), act),
            pltpu.VMEM((2, frames, channels, columns), act),
            pltpu.VMEM((2, frames, channels, columns), act),
            pltpu.VMEM((2, 2, rows, channels, columns), act),
            pltpu.VMEM((2, 2, channels, columns), act),
            pltpu.VMEM((2, 2, channels, columns), act),
            pltpu.VMEM((frames + 2, rows + 2, 3, channels, columns), act),
            pltpu.VMEM((frames + 2, rows + 2, 3, channels, columns), act),
            pltpu.VMEM((2, 2, 2 * channels, 2 * columns), jnp.float32),
            pltpu.SemaphoreType.DMA((2, 9)),
            pltpu.SemaphoreType.DMA((2, 9)),
            pltpu.SemaphoreType.DMA((6,)),
        ],
        compiler_params=pltpu.CompilerParams(
            collective_id=0, has_side_effects=True, vmem_limit_bytes=53 * 1024 * 1024
        ),
        cost_estimate=pl.CostEstimate(
            flops=2 * cells, bytes_accessed=3 * features.size * 2, transcendentals=features.size * 4
        ),
    )(by_row, first_weight, second_weight, *vectors)
    return jnp.transpose(result, (2, 0, 1, 3))


def solution(mesh):
    return jax.shard_map(
        local,
        mesh=mesh,
        in_specs=(P(None, "tm", "height", None), P(), P(), P(), P(), P(), P()),
        out_specs=P(None, "tm", "height", None),
        check_vma=False,
    )
```

profile of v0, /device:TPU:11, one launch (start us, length us, event | category | flops | bytes accessed | tf_op | source)
XLA Modules:
  0.0 20.5 jit_solution(1626853732710482541)
XLA Ops:
  0.0 0.0 copy-start.3
  0.0 1.1 %copy.11 = bf16[96,4,4,128]{3,0,2,1:T(8,128)(2,1)S(1)} copy(bf16[96,4,4,128]{3,2,1,0:T(4,128)(2,1)} %param.7) | data formatting | bytes 786432 | tf_op args[0]
  1.1 0.0 copy-start
  1.1 0.0 copy-start.1
  1.1 0.0 copy-start.2
  1.2 0.0 copy-done.3
  1.2 0.6 %copy-done = f32[96]{0:T(128)S(1)} copy-done((f32[96]{0:T(128)S(1)}, f32[96]{0:T(128)}, u32[]{:S(2)}) %copy-start) | copy-done | bytes 408
  1.8 0.0 copy-done.1
  1.8 0.0 copy-done.2
  1.8 17.8 %shard_map.73 = bf16[4,4,96,128]{3,2,1,0:T(8,128)(2,1)S(1)} custom-call(bf16[4,4,96,128]{3,2,1,0:T(8,128)(2,1)S(1)} %bitcast.9, bf16[96,2592]{1,0:T(8,128)(2,1)} %first_weight_hbm.1, bf16[96,2592]{1,0:T(8,128)(2,1)} %second_weight_hbm.1, f32[1,96]{1,0:T(1,128)S(1)} %bitcast.10, f32[1,96]{1,0:T(1,128)S(1)} %bitcast.11, f32[1,96]{1,0:T(1,128)S(1)} %bitcast.12, ...), custom_call_target="tpu_custom_call" | custom-call | flops 2038431744 | bytes 1179648 | tf_op jit(solution)/shard_map/pallas_call | solution.py:424
  19.6 0.9 %copy.9 = bf16[96,4,4,128]{3,2,1,0:T(4,128)(2,1)} copy(bf16[96,4,4,128]{3,0,2,1:T(8,128)(2,1)S(1)} %bitcast.8) | data formatting | bytes 786432 | tf_op jit(solution)/shard_map/transpose | solution.py:455
Async XLA Ops:
  0.0 1.2 %copy-start.3 = (f32[96]{0:T(128)S(1)}, f32[96]{0:T(128)}, u32[]{:S(2)}) copy-start(f32[96]{0:T(128)} %param.13) | copy-start | bytes 1156
  1.1 0.7 %copy-start = (f32[96]{0:T(128)S(1)}, f32[96]{0:T(128)}, u32[]{:S(2)}) copy-start(f32[96]{0:T(128)} %param.8) | copy-start | bytes 1156
  1.1 0.7 %copy-start.1 = (f32[96]{0:T(128)S(1)}, f32[96]{0:T(128)}, u32[]{:S(2)}) copy-start(f32[96]{0:T(128)} %param.10) | copy-start | bytes 1156
  1.1 0.7 %copy-start.2 = (f32[96]{0:T(128)S(1)}, f32[96]{0:T(128)}, u32[]{:S(2)}) copy-start(f32[96]{0:T(128)} %param.11) | copy-start | bytes 1156
where the time goes:
time: 20.8 us; the launch traced here: 20.5 us
  Pallas kernels  17.8 us (86%)
  local copies, waits for them, and re-layouts  2.72 us (13%)
    pallas_call x1, Pallas kernels, local(): pl.pallas_call(functools.partial(kernel, lax.axis_size('tm'), lax.axis_si...  17.8 us
    unnamed x9, local copies, waits for them, and re-layouts  1.77 us
    transpose x1, local copies, waits for them, and re-layouts, local(): return jnp.transpose(result, (2, 0, 1, 3))  0.95 us

commit v1 on v0

--- a/solution.py
+++ b/solution.py
@@ -84,6 +84,7 @@
     earlier,
     earlier_above,
     earlier_below,
+    partial,
     taps_a,
     taps_b,
     total,
@@ -154,7 +155,7 @@
         return message(
             layer,
             4 + part,
-            own.at[layer, pl.ds(2, 2), rows],
+            partial.at[:, rows] if layer else own.at[layer, pl.ds(2, 2), rows],
             earlier.at[layer, :, rows],
             later,
         )
@@ -309,6 +310,8 @@
     def first_late(k, pair):
         @pl.when(k == 1)
         def _():
+            loads[5].wait()
+            stack(weights_b, second_weight)
             take_rows(0, taps_a, 1)
             take_rows(0, taps_a, 0)
 
@@ -316,27 +319,35 @@
         part = part + multiply(weights_a[:two, :], taps_a, 4, pair)
         second_activation(2, pair, plus_bias(part, first_bias))
 
-        @pl.when(k == 0)
-        def _():
-            send_later(1, (2,))
-
     each_pair(first_late)
-    send_later(1, (0, 1))
     send_rows(1, 1)
-    pass_on(0)
+
+    def second_late(k, pair):
+        @pl.when(has_next)
+        def _():
+            part = multiply(weights_b[...], taps_b, 4, pair)
+            total[1, k] = plus_bias(part[:two, :], second_bias)
+            for i in range(2):
+                for j, r in enumerate(pair):
+                    partial[i, r] = cut(part, 2 + i, j).astype(jnp.bfloat16)
+
+        @pl.when(jnp.logical_not(has_next))
+        def _():
+            part = multiply(weights_b[:two, :], taps_b, 4, pair)
+            total[1, k] = plus_bias(part, second_bias)
+
+    second_late(0, (1, 2))
+    send_later(1, (2,))
 
     def first_early(k, pair):
         total[0, k] = plus_bias(multiply(weights_a[:two, :], taps_a, 2, pair), first_bias)
 
     each_pair(first_early)
 
-    loads[5].wait()
-    stack(weights_b, second_weight)
-
-    def second_late(k, pair):
-        total[1, k] = plus_bias(multiply(weights_b[:two, :], taps_b, 4, pair), second_bias)
-
-    second_late(0, (1, 2))
+    pass_on(0)
+    take_rows(1, taps_b, 1)
+    second_late(1, (0, 3))
+    send_later(1, (0, 1))
 
     @pl.when(has_prev)
     def _():
@@ -355,37 +366,38 @@
 
     each_pair(first_earlier)
     send_rows(1, 0)
-    take_rows(1, taps_b, 1)
-    second_late(1, (0, 3))
 
     def second_early(k, pair):
         @pl.when(k == 1)
         def _():
-            pass_on(1)
             take_rows(1, taps_b, 0)
 
         part = multiply(weights_b[...], taps_b, 2, pair)
         finish(2, pair, total[1, k] + part[two:, :])
         total[0, k] = plus_bias(part[:two, :], second_bias)
 
-    each_pair(second_early)
-
-    @pl.when(has_prev)
-    def _():
-        take_earlier(1, taps_b)
-
-    def second_earlier(k, pair):
         @pl.when(has_prev)
         def _():
+            @pl.when(k == 0)
+            def _():
+                to_later(1, 2).wait_recv()
+
             @pl.when(k == 1)
             def _():
-                take_corners(1, taps_b)
-
-            total[0, k] += multiply(weights_b[two:, :], taps_b, 0, pair)
+                to_later(1, 0).wait_recv()
+                to_later(1, 1).wait_recv()
+
+            for i in range(2):
+                for j, r in enumerate(pair):
+                    block = (
+                        pl.ds(i * channels, channels),
+                        pl.ds(j * columns, columns),
+                    )
+                    total[0, k, *block] += earlier[1, i, r].astype(jnp.float32)
 
         finish(0, pair, total[0, k])
 
-    each_pair(second_earlier)
+    each_pair(second_early)
 
     for layer in range(2):
 
@@ -404,13 +416,13 @@
             for part in range(3):
                 to_later(layer, part).wait_send()
 
-        @pl.when(has_prev & has_up)
-        def _():
-            pass_up(layer).wait_send()
-
-        @pl.when(has_prev & has_down)
-        def _():
-            pass_down(layer).wait_send()
+    @pl.when(has_prev & has_up)
+    def _():
+        pass_up(0).wait_send()
+
+    @pl.when(has_prev & has_down)
+    def _():
+        pass_down(0).wait_send()
 
 
 def local(features, first_gain, first_weight, first_bias, second_gain, second_weight, second_bias):
@@ -438,6 +450,7 @@
             pltpu.VMEM((2, 2, rows, channels, columns), act),
             pltpu.VMEM((2, 2, channels, columns), act),
             pltpu.VMEM((2, 2, channels, columns), act),
+            pltpu.VMEM((2, rows, channels, columns), act),
             pltpu.VMEM((frames + 2, rows + 2, 3, channels, columns), act),
             pltpu.VMEM((frames + 2, rows + 2, 3, channels, columns), act),
             pltpu.VMEM((2, 2, 2 * channels, 2 * columns), jnp.float32),

time: 20.8 us -> 19.1 us (0.918)
  Pallas kernels: 17.8 us -> 16.1 us
    pallas_call x1, Pallas kernels: 17.8 us -> 16.1 us  [local(): pl.pallas_call(functools.partial(kernel, lax.axis_size('tm'), lax.axis_si...]
where the time goes in v1:
time: 19.1 us; the launch traced here: 18.9 us
  Pallas kernels  16.1 us (84%)
  local copies, waits for them, and re-layouts  2.72 us (14%)
    pallas_call x1, Pallas kernels, local(): pl.pallas_call(functools.partial(kernel, lax.axis_size('tm'), lax.axis_si...  16.1 us
    unnamed x9, local copies, waits for them, and re-layouts  1.77 us
    transpose x1, local copies, waits for them, and re-layouts, local(): return jnp.transpose(result, (2, 0, 1, 3))  0.95 us

profile of v1, /device:TPU:11, one launch (start us, length us, event | category | flops | bytes accessed | tf_op | source)
XLA Modules:
  0.0 18.9 jit_solution(16571621819214409079)
XLA Ops:
  0.0 0.0 copy-start.3
  0.0 1.1 %copy.11 = bf16[96,4,4,128]{3,0,2,1:T(8,128)(2,1)S(1)} copy(bf16[96,4,4,128]{3,2,1,0:T(4,128)(2,1)} %param.7) | data formatting | bytes 786432 | tf_op args[0]
  1.1 0.0 copy-start
  1.1 0.0 copy-start.1
  1.1 0.0 copy-start.2
  1.2 0.0 copy-done.3
  1.2 0.6 %copy-done = f32[96]{0:T(128)S(1)} copy-done((f32[96]{0:T(128)S(1)}, f32[96]{0:T(128)}, u32[]{:S(2)}) %copy-start) | copy-done | bytes 408
  1.8 0.0 copy-done.1
  1.8 0.0 copy-done.2
  1.8 16.1 %shard_map.73 = bf16[4,4,96,128]{3,2,1,0:T(8,128)(2,1)S(1)} custom-call(bf16[4,4,96,128]{3,2,1,0:T(8,128)(2,1)S(1)} %bitcast.9, bf16[96,2592]{1,0:T(8,128)(2,1)} %first_weight_hbm.1, bf16[96,2592]{1,0:T(8,128)(2,1)} %second_weight_hbm.1, f32[1,96]{1,0:T(1,128)S(1)} %bitcast.10, f32[1,96]{1,0:T(1,128)S(1)} %bitcast.11, f32[1,96]{1,0:T(1,128)S(1)} %bitcast.12, ...), custom_call_target="tpu_custom_call" | custom-call | flops 2038431744 | bytes 1179648 | tf_op jit(solution)/shard_map/pallas_call | solution.py:436
  17.9 0.9 %copy.9 = bf16[96,4,4,128]{3,2,1,0:T(4,128)(2,1)} copy(bf16[96,4,4,128]{3,0,2,1:T(8,128)(2,1)S(1)} %bitcast.8) | data formatting | bytes 786432 | tf_op jit(solution)/shard_map/transpose | solution.py:468
Async XLA Ops:
  0.0 1.2 %copy-start.3 = (f32[96]{0:T(128)S(1)}, f32[96]{0:T(128)}, u32[]{:S(2)}) copy-start(f32[96]{0:T(128)} %param.13) | copy-start | bytes 1156
  1.1 0.7 %copy-start = (f32[96]{0:T(128)S(1)}, f32[96]{0:T(128)}, u32[]{:S(2)}) copy-start(f32[96]{0:T(128)} %param.8) | copy-start | bytes 1156
  1.1 0.7 %copy-start.1 = (f32[96]{0:T(128)S(1)}, f32[96]{0:T(128)}, u32[]{:S(2)}) copy-start(f32[96]{0:T(128)} %param.10) | copy-start | bytes 1156
  1.1 0.7 %copy-start.2 = (f32[96]{0:T(128)S(1)}, f32[96]{0:T(128)}, u32[]{:S(2)}) copy-start(f32[96]{0:T(128)} %param.11) | copy-start | bytes 1156

commit v2 on v1

--- a/solution.py
+++ b/solution.py
@@ -137,14 +137,20 @@
             device_id_type=MESH,
         )
 
+    def halves(layer):
+        return range(2) if layer else range(1)
+
+    def span(layer, half):
+        return pl.ds(2 * half, 2) if layer else pl.ds(0, 4)
+
     def to_up(layer, half):
-        frames = pl.ds(2 * half, 2)
+        frames = span(layer, half)
         return message(
             layer, half, own.at[layer, frames, 0], below.at[layer, frames], up
         )
 
     def to_down(layer, half):
-        frames = pl.ds(2 * half, 2)
+        frames = span(layer, half)
         return message(
             layer, 2 + half, own.at[layer, frames, 3], above.at[layer, frames], down
         )
@@ -185,25 +191,26 @@
         for frame in frames:
             taps[frame, row] = jnp.zeros(taps.shape[2:], taps.dtype)
 
-    def spread_frames(taps, first, row, source):
+    def spread_frames(taps, first, row, source, count=2):
         def step(f, carry):
             spread(taps, first + f, row, source[f])
             return carry
 
-        lax.fori_loop(0, 2, step, 0)
+        lax.fori_loop(0, count, step, 0)
 
     def take_rows(layer, taps, half):
-        frames = pl.ds(2 * half, 2)
+        frames = span(layer, half)
+        count = 2 if layer else 4
 
         @pl.when(has_up)
         def _():
             to_down(layer, half).wait_recv()
-            spread_frames(taps, 2 + 2 * half, 0, above.at[layer, frames])
+            spread_frames(taps, 2 + 2 * half, 0, above.at[layer, frames], count)
 
         @pl.when(has_down)
         def _():
             to_up(layer, half).wait_recv()
-            spread_frames(taps, 2 + 2 * half, 5, below.at[layer, frames])
+            spread_frames(taps, 2 + 2 * half, 5, below.at[layer, frames], count)
 
     def clear_edges(taps):
         @pl.when(jnp.logical_not(has_up))
@@ -272,22 +279,27 @@
         column(vectors, i, columns) for i in range(4)
     )
 
-    def first_activation(f, carry):
-        for r in range(4):
-            act = activate(features[f, r].astype(jnp.float32), first_gain)
-            own[0, f, r] = act.astype(jnp.bfloat16)
-            spread(taps_a, f + 2, r + 1, act)
-        return carry
-
-    lax.fori_loop(0, 4, first_activation, 0)
-
+    def first_activation(rows):
+        def step(half, carry):
+            for i in range(2):
+                f = 2 * half + i
+                for r in rows:
+                    act = activate(features[f, r].astype(jnp.float32), first_gain)
+                    own[0, f, r] = act.astype(jnp.bfloat16)
+                    spread(taps_a, f + 2, r + 1, act)
+            return carry
+
+        lax.fori_loop(0, 2, step, 0)
+
+    first_activation((0, 3))
     pl.semaphore_wait(
         barrier,
         sum(present.astype(jnp.int32) for present, _ in neighbours),
     )
-    send_rows(0, 1)
     send_rows(0, 0)
-    send_later(0, (0, 1, 2))
+    send_later(0, (0, 1))
+    first_activation((1, 2))
+    send_later(0, (2,))
 
     loads[4].wait()
     stack(weights_a, first_weight)
@@ -312,11 +324,11 @@
         def _():
             loads[5].wait()
             stack(weights_b, second_weight)
-            take_rows(0, taps_a, 1)
             take_rows(0, taps_a, 0)
 
-        part = multiply(weights_a[two:, :], taps_a, 2, pair)
-        part = part + multiply(weights_a[:two, :], taps_a, 4, pair)
+        both = multiply(weights_a[...], taps_a, 2, pair)
+        total[0, k] = plus_bias(both[:two, :], first_bias)
+        part = both[two:, :] + multiply(weights_a[:two, :], taps_a, 4, pair)
         second_activation(2, pair, plus_bias(part, first_bias))
 
     each_pair(first_late)
@@ -338,11 +350,6 @@
 
     second_late(0, (1, 2))
     send_later(1, (2,))
-
-    def first_early(k, pair):
-        total[0, k] = plus_bias(multiply(weights_a[:two, :], taps_a, 2, pair), first_bias)
-
-    each_pair(first_early)
 
     pass_on(0)
     take_rows(1, taps_b, 1)
@@ -403,12 +410,12 @@
 
         @pl.when(has_up)
         def _():
-            for half in range(2):
+            for half in halves(layer):
                 to_up(layer, half).wait_send()
 
         @pl.when(has_down)
         def _():
-            for half in range(2):
+            for half in halves(layer):
                 to_down(layer, half).wait_send()
 
         @pl.when(has_next)

time: 19.1 us -> 19.4 us (1.016)
  Pallas kernels: 16.1 us -> 16.5 us
    pallas_call x1, Pallas kernels: 16.1 us -> 16.5 us  [local(): pl.pallas_call(functools.partial(kernel, lax.axis_size('tm'), lax.axis_si...]
where the time goes in v2:
time: 19.4 us; the launch traced here: 19.3 us
  Pallas kernels  16.5 us (85%)
  local copies, waits for them, and re-layouts  2.72 us (14%)
    pallas_call x1, Pallas kernels, local(): pl.pallas_call(functools.partial(kernel, lax.axis_size('tm'), lax.axis_si...  16.5 us
    unnamed x9, local copies, waits for them, and re-layouts  1.77 us
    transpose x1, local copies, waits for them, and re-layouts, local(): return jnp.transpose(result, (2, 0, 1, 3))  0.95 us

profile of v2, /device:TPU:11, one launch (start us, length us, event | category | flops | bytes accessed | tf_op | source)
XLA Modules:
  0.0 19.3 jit_solution(11565077508700360997)
XLA Ops:
  0.0 0.0 copy-start.3
  0.0 1.1 %copy.11 = bf16[96,4,4,128]{3,0,2,1:T(8,128)(2,1)S(1)} copy(bf16[96,4,4,128]{3,2,1,0:T(4,128)(2,1)} %param.7) | data formatting | bytes 786432 | tf_op args[0]
  1.1 0.0 copy-start
  1.1 0.0 copy-start.1
  1.1 0.0 copy-start.2
  1.2 0.0 copy-done.3
  1.2 0.6 %copy-done = f32[96]{0:T(128)S(1)} copy-done((f32[96]{0:T(128)S(1)}, f32[96]{0:T(128)}, u32[]{:S(2)}) %copy-start) | copy-done | bytes 408
  1.8 0.0 copy-done.1
  1.8 0.0 copy-done.2
  1.8 16.5 %shard_map.73 = bf16[4,4,96,128]{3,2,1,0:T(8,128)(2,1)S(1)} custom-call(bf16[4,4,96,128]{3,2,1,0:T(8,128)(2,1)S(1)} %bitcast.9, bf16[96,2592]{1,0:T(8,128)(2,1)} %first_weight_hbm.1, bf16[96,2592]{1,0:T(8,128)(2,1)} %second_weight_hbm.1, f32[1,96]{1,0:T(1,128)S(1)} %bitcast.10, f32[1,96]{1,0:T(1,128)S(1)} %bitcast.11, f32[1,96]{1,0:T(1,128)S(1)} %bitcast.12, ...), custom_call_target="tpu_custom_call" | custom-call | flops 2038431744 | bytes 1179648 | tf_op jit(solution)/shard_map/pallas_call | solution.py:443
  18.3 0.9 %copy.9 = bf16[96,4,4,128]{3,2,1,0:T(4,128)(2,1)} copy(bf16[96,4,4,128]{3,0,2,1:T(8,128)(2,1)S(1)} %bitcast.8) | data formatting | bytes 786432 | tf_op jit(solution)/shard_map/transpose | solution.py:475
Async XLA Ops:
  0.0 1.2 %copy-start.3 = (f32[96]{0:T(128)S(1)}, f32[96]{0:T(128)}, u32[]{:S(2)}) copy-start(f32[96]{0:T(128)} %param.13) | copy-start | bytes 1156
  1.1 0.7 %copy-start = (f32[96]{0:T(128)S(1)}, f32[96]{0:T(128)}, u32[]{:S(2)}) copy-start(f32[96]{0:T(128)} %param.8) | copy-start | bytes 1156
  1.1 0.7 %copy-start.1 = (f32[96]{0:T(128)S(1)}, f32[96]{0:T(128)}, u32[]{:S(2)}) copy-start(f32[96]{0:T(128)} %param.10) | copy-start | bytes 1156
  1.1 0.7 %copy-start.2 = (f32[96]{0:T(128)S(1)}, f32[96]{0:T(128)}, u32[]{:S(2)}) copy-start(f32[96]{0:T(128)} %param.11) | copy-start | bytes 1156

commit v3 on v1

--- a/solution.py
+++ b/solution.py
@@ -345,9 +345,17 @@
     each_pair(first_early)
 
     pass_on(0)
-    take_rows(1, taps_b, 1)
-    second_late(1, (0, 3))
-    send_later(1, (0, 1))
+
+    def finish_late():
+        take_rows(1, taps_b, 1)
+        second_late(1, (0, 3))
+        send_later(1, (0, 1))
+
+    between = has_prev & has_next
+
+    @pl.when(between)
+    def _():
+        finish_late()
 
     @pl.when(has_prev)
     def _():
@@ -366,6 +374,10 @@
 
     each_pair(first_earlier)
     send_rows(1, 0)
+
+    @pl.when(jnp.logical_not(between))
+    def _():
+        finish_late()
 
     def second_early(k, pair):
         @pl.when(k == 1)

time: 19.1 us -> 18.7 us (0.979)
  Pallas kernels: 16.1 us -> 15.8 us
    pallas_call x1, Pallas kernels: 16.1 us -> 15.8 us  [local(): pl.pallas_call(functools.partial(kernel, lax.axis_size('tm'), lax.axis_si...]
where the time goes in v3:
time: 18.7 us; the launch traced here: 18.5 us
  Pallas kernels  15.8 us (84%)
  local copies, waits for them, and re-layouts  2.72 us (15%)
    pallas_call x1, Pallas kernels, local(): pl.pallas_call(functools.partial(kernel, lax.axis_size('tm'), lax.axis_si...  15.8 us
    unnamed x9, local copies, waits for them, and re-layouts  1.77 us
    transpose x1, local copies, waits for them, and re-layouts, local(): return jnp.transpose(result, (2, 0, 1, 3))  0.95 us

profile of v3, /device:TPU:11, one launch (start us, length us, event | category | flops | bytes accessed | tf_op | source)
XLA Modules:
  0.0 18.5 jit_solution(14062963101727322552)
XLA Ops:
  0.0 0.0 copy-start.3
  0.0 1.1 %copy.11 = bf16[96,4,4,128]{3,0,2,1:T(8,128)(2,1)S(1)} copy(bf16[96,4,4,128]{3,2,1,0:T(4,128)(2,1)} %param.7) | data formatting | bytes 786432 | tf_op args[0]
  1.1 0.0 copy-start
  1.1 0.0 copy-start.1
  1.1 0.0 copy-start.2
  1.2 0.0 copy-done.3
  1.2 0.6 %copy-done = f32[96]{0:T(128)S(1)} copy-done((f32[96]{0:T(128)S(1)}, f32[96]{0:T(128)}, u32[]{:S(2)}) %copy-start) | copy-done | bytes 408
  1.8 0.0 copy-done.1
  1.8 0.0 copy-done.2
  1.8 15.8 %shard_map.73 = bf16[4,4,96,128]{3,2,1,0:T(8,128)(2,1)S(1)} custom-call(bf16[4,4,96,128]{3,2,1,0:T(8,128)(2,1)S(1)} %bitcast.9, bf16[96,2592]{1,0:T(8,128)(2,1)} %first_weight_hbm.1, bf16[96,2592]{1,0:T(8,128)(2,1)} %second_weight_hbm.1, f32[1,96]{1,0:T(1,128)S(1)} %bitcast.10, f32[1,96]{1,0:T(1,128)S(1)} %bitcast.11, f32[1,96]{1,0:T(1,128)S(1)} %bitcast.12, ...), custom_call_target="tpu_custom_call" | custom-call | flops 2038431744 | bytes 1179648 | tf_op jit(solution)/shard_map/pallas_call | solution.py:448
  17.6 0.9 %copy.9 = bf16[96,4,4,128]{3,2,1,0:T(4,128)(2,1)} copy(bf16[96,4,4,128]{3,0,2,1:T(8,128)(2,1)S(1)} %bitcast.8) | data formatting | bytes 786432 | tf_op jit(solution)/shard_map/transpose | solution.py:480
Async XLA Ops:
  0.0 1.2 %copy-start.3 = (f32[96]{0:T(128)S(1)}, f32[96]{0:T(128)}, u32[]{:S(2)}) copy-start(f32[96]{0:T(128)} %param.13) | copy-start | bytes 1156
  1.1 0.7 %copy-start = (f32[96]{0:T(128)S(1)}, f32[96]{0:T(128)}, u32[]{:S(2)}) copy-start(f32[96]{0:T(128)} %param.8) | copy-start | bytes 1156
  1.1 0.7 %copy-start.1 = (f32[96]{0:T(128)S(1)}, f32[96]{0:T(128)}, u32[]{:S(2)}) copy-start(f32[96]{0:T(128)} %param.10) | copy-start | bytes 1156
  1.1 0.7 %copy-start.2 = (f32[96]{0:T(128)S(1)}, f32[96]{0:T(128)}, u32[]{:S(2)}) copy-start(f32[96]{0:T(128)} %param.11) | copy-start | bytes 1156

commit v4 on v3

--- a/solution.py
+++ b/solution.py
@@ -339,12 +339,13 @@
     second_late(0, (1, 2))
     send_later(1, (2,))
 
+    pass_on(0)
+
     def first_early(k, pair):
         total[0, k] = plus_bias(multiply(weights_a[:two, :], taps_a, 2, pair), first_bias)
 
     each_pair(first_early)
 
-    pass_on(0)
 
     def finish_late():
         take_rows(1, taps_b, 1)

time: 18.7 us -> 18.9 us (1.011)
  Pallas kernels: 15.8 us -> 16 us
    pallas_call x1, Pallas kernels: 15.8 us -> 16 us  [local(): pl.pallas_call(functools.partial(kernel, lax.axis_size('tm'), lax.axis_si...]
where the time goes in v4:
time: 18.9 us; the launch traced here: 18.8 us
  Pallas kernels  16 us (85%)
  local copies, waits for them, and re-layouts  2.72 us (14%)
    pallas_call x1, Pallas kernels, local(): pl.pallas_call(functools.partial(kernel, lax.axis_size('tm'), lax.axis_si...  16 us
    unnamed x9, local copies, waits for them, and re-layouts  1.77 us
    transpose x1, local copies, waits for them, and re-layouts, local(): return jnp.transpose(result, (2, 0, 1, 3))  0.95 us

profile of v4, /device:TPU:11, one launch (start us, length us, event | category | flops | bytes accessed | tf_op | source)
XLA Modules:
  0.0 18.8 jit_solution(18091705581809272902)
XLA Ops:
  0.0 0.0 copy-start.3
  0.0 1.1 %copy.11 = bf16[96,4,4,128]{3,0,2,1:T(8,128)(2,1)S(1)} copy(bf16[96,4,4,128]{3,2,1,0:T(4,128)(2,1)} %param.7) | data formatting | bytes 786432 | tf_op args[0]
  1.1 0.0 copy-start
  1.1 0.0 copy-start.1
  1.1 0.0 copy-start.2
  1.2 0.0 copy-done.3
  1.2 0.6 %copy-done = f32[96]{0:T(128)S(1)} copy-done((f32[96]{0:T(128)S(1)}, f32[96]{0:T(128)}, u32[]{:S(2)}) %copy-start) | copy-done | bytes 408
  1.8 0.0 copy-done.1
  1.8 0.0 copy-done.2
  1.8 16.0 %shard_map.73 = bf16[4,4,96,128]{3,2,1,0:T(8,128)(2,1)S(1)} custom-call(bf16[4,4,96,128]{3,2,1,0:T(8,128)(2,1)S(1)} %bitcast.9, bf16[96,2592]{1,0:T(8,128)(2,1)} %first_weight_hbm.1, bf16[96,2592]{1,0:T(8,128)(2,1)} %second_weight_hbm.1, f32[1,96]{1,0:T(1,128)S(1)} %bitcast.10, f32[1,96]{1,0:T(1,128)S(1)} %bitcast.11, f32[1,96]{1,0:T(1,128)S(1)} %bitcast.12, ...), custom_call_target="tpu_custom_call" | custom-call | flops 2038431744 | bytes 1179648 | tf_op jit(solution)/shard_map/pallas_call | solution.py:449
  17.8 0.9 %copy.9 = bf16[96,4,4,128]{3,2,1,0:T(4,128)(2,1)} copy(bf16[96,4,4,128]{3,0,2,1:T(8,128)(2,1)S(1)} %bitcast.8) | data formatting | bytes 786432 | tf_op jit(solution)/shard_map/transpose | solution.py:481
Async XLA Ops:
  0.0 1.2 %copy-start.3 = (f32[96]{0:T(128)S(1)}, f32[96]{0:T(128)}, u32[]{:S(2)}) copy-start(f32[96]{0:T(128)} %param.13) | copy-start | bytes 1156
  1.1 0.7 %copy-start = (f32[96]{0:T(128)S(1)}, f32[96]{0:T(128)}, u32[]{:S(2)}) copy-start(f32[96]{0:T(128)} %param.8) | copy-start | bytes 1156
  1.1 0.7 %copy-start.1 = (f32[96]{0:T(128)S(1)}, f32[96]{0:T(128)}, u32[]{:S(2)}) copy-start(f32[96]{0:T(128)} %param.10) | copy-start | bytes 1156
  1.1 0.7 %copy-start.2 = (f32[96]{0:T(128)S(1)}, f32[96]{0:T(128)}, u32[]{:S(2)}) copy-start(f32[96]{0:T(128)} %param.11) | copy-start | bytes 1156
